TPU v7x, 128 devices: a whole 4x4x4 slice. The times are simulated.
128 devices in a mesh: tile: 8 (over z, y_lo), pos: 16 (over y_hi, x, core).
Axes of the slice: x: 4, y: 4 (y_hi: 2, y_lo: 2; y = y_hi * 2 + y_lo), z: 4, core: 2. Of those that a mesh axis runs over, the one named last changes fastest.
Arguments:
- object_field: float32 [2, 4096, 8192], P(None, 'tile', 'pos'), may hold values from -5 to 5
- probe_field: float32 [2, 512, 512], replicated, may hold values from -5 to 5
- offsets: int32 [8, 16, 3, 2], P('tile', 'pos'), may hold values from 0 to 511, as said below
- counts: int32 [8, 16], P('tile'), may hold values from 1 to 3, as said below
- intensity: float32 [8, 16, 3, 512, 512], P('tile', 'pos'), may hold values from 0 to 2
Outputs:
- object_grad: float32 [2, 4096, 8192], P(None, 'tile', 'pos')
- probe_grad: float32 [2, 512, 512], replicated
Inputs may be any that keep to these rules, and one draw needn't show every extreme that they name: `offsets`: offsets are local to the device's block. On the last index of tile the row offset is at most 0, on the last index of pos the column offset likewise, so every window lies inside the object. Offsets of unused slots are drawn too and mean nothing. `counts`: some device uses all 3 slots and some uses one; the used slots of a device are its first ones.
All inputs are finite; a program needn't handle non-finite values.
Results may differ from a plain program's by a relative error of at most 0.0003.
Values sent between devices are 32-bit elements; how exact they have to be, the bound alone decides.
A program may use at most 128 MiB of HBM per device.

v0:
```python
import math

import jax
import jax.numpy as jnp
from jax import lax
from jax.sharding import PartitionSpec as P


def passed_along(x, axis, by):
    length = lax.axis_size(axis)
    pairs = [(i, i + by) for i in range(length) if 0 <= i + by < length]
    return lax.ppermute(x, axis, pairs)


def dft_tables(length):
    points = jnp.arange(length, dtype=jnp.int32)
    phases = points[:, None] * points[None, :] % length
    angles = phases.astype(jnp.float32) * (2.0 * math.pi / length)
    factor = 1.0 / math.sqrt(length)
    return (jnp.cos(angles) * factor, jnp.sin(angles) * factor)


def matmul(left_op, right_op):
    return jnp.dot(
        left_op, right_op, precision=lax.Precision.HIGHEST, preferred_element_type=jnp.float32
    )


def apply_left(cosine, sine, real_part, imag_part, sign):
    length = real_part.shape[1]
    joined = jnp.concatenate([real_part, imag_part], axis=1)
    cos_prod = matmul(cosine, joined)
    sin_prod = matmul(sine, joined)
    return (
        cos_prod[:, :length] + sign * sin_prod[:, length:],
        cos_prod[:, length:] - sign * sin_prod[:, :length],
    )


def apply_right(cosine, sine, real_part, imag_part, sign):
    length = real_part.shape[0]
    joined = jnp.concatenate([real_part, imag_part], axis=0)
    cos_prod = matmul(joined, cosine)
    sin_prod = matmul(joined, sine)
    return (
        cos_prod[:length] + sign * sin_prod[length:],
        cos_prod[length:] - sign * sin_prod[:length],
    )


def slot_terms(patch_now, probe_field, measured, cosine, sine):
    probe_real = probe_field[0]
    probe_imag = probe_field[1]
    wave_real = probe_real * patch_now[0] - probe_imag * patch_now[1]
    wave_imag = probe_real * patch_now[1] + probe_imag * patch_now[0]
    spec_real, spec_imag = apply_left(cosine, sine, wave_real, wave_imag, 1.0)
    spec_real, spec_imag = apply_right(cosine, sine, spec_real, spec_imag, 1.0)
    mismatch = spec_real * spec_real + spec_imag * spec_imag - measured
    back_real, back_imag = apply_left(
        cosine, sine, mismatch * spec_real, mismatch * spec_imag, -1.0
    )
    back_real, back_imag = apply_right(cosine, sine, back_real, back_imag, -1.0)
    object_term = jnp.stack(
        [
            probe_real * back_real + probe_imag * back_imag,
            probe_real * back_imag - probe_imag * back_real,
        ]
    )
    probe_term = jnp.stack(
        [
            patch_now[0] * back_real + patch_now[1] * back_imag,
            patch_now[0] * back_imag - patch_now[1] * back_real,
        ]
    )
    return (object_term, probe_term)


def run_items(patches, measured, probe_field, cosine, sine, item_slot, item_live, step_count):

    def one_item(step, state):
        slot_pick = item_slot(step)

        def compute(inner):
            object_term, probe_term = slot_terms(
                patches[slot_pick], probe_field, measured[slot_pick], cosine, sine
            )
            return (inner[0].at[slot_pick].set(object_term), inner[1] + probe_term)

        def untouched(inner):
            return inner

        return lax.cond(item_live(step), compute, untouched, state)

    start_state = (jnp.zeros(patches.shape, jnp.float32), jnp.zeros(probe_field.shape, jnp.float32))
    return lax.fori_loop(0, step_count, one_item, start_state)


def on_device(object_field, probe_field, offsets, counts, intensity):
    window = probe_field.shape[1]
    block_rows = object_field.shape[1]
    block_cols = object_field.shape[2]
    slot_count = offsets.shape[2]
    right_rim = passed_along(object_field, "pos", -1)
    widened = jnp.concatenate([object_field, right_rim], axis=2)
    lower_rim = passed_along(widened, "tile", -1)
    extended = jnp.concatenate([widened, lower_rim], axis=1)
    local_offsets = offsets.reshape(slot_count, 2)
    measured = intensity.reshape(slot_count, window, window)
    count_row = counts.reshape(-1)
    position_index = lax.axis_index("pos")
    own_count = count_row[position_index]
    zero_int = jnp.zeros((), jnp.int32)

    def cut_patch(offset_pair):
        return lax.dynamic_slice(
            extended, (zero_int, offset_pair[0], offset_pair[1]), (2, window, window)
        )

    patches = jax.vmap(cut_patch)(local_offsets)
    cosine, sine = dft_tables(window)
    own_terms, probe_sum = run_items(
        patches,
        measured,
        probe_field,
        cosine,
        sine,
        lambda step: step,
        lambda step: step < own_count,
        slot_count,
    )

    def place_term(slot, grad_buffer):
        offset_pair = local_offsets[slot]
        corner = (zero_int, offset_pair[0], offset_pair[1])
        current = lax.dynamic_slice(grad_buffer, corner, (2, window, window))
        return lax.dynamic_update_slice(grad_buffer, current + own_terms[slot], corner)

    grad_buffer = lax.fori_loop(0, slot_count, place_term, jnp.zeros(extended.shape, jnp.float32))
    lower_back = passed_along(grad_buffer[:, block_rows:, :], "tile", 1)
    grad_buffer = grad_buffer.at[:, :window, :].add(lower_back)
    right_back = passed_along(grad_buffer[:, :block_rows, block_cols:], "pos", 1)
    object_grad = grad_buffer[:, :block_rows, :block_cols].at[:, :, :window].add(right_back)
    probe_total = lax.psum(probe_sum, ("tile", "pos"))
    probe_grad = probe_total * (1.0 / (lax.axis_size("tile") * lax.axis_size("pos") * slot_count))
    return (object_grad, probe_grad)


def solution(mesh):
    placed = (
        P(None, "tile", "pos"),
        P(),
        P("tile", "pos", None, None),
        P("tile", None),
        P("tile", "pos", None, None, None),
    )
    return jax.shard_map(
        on_device,
        mesh=mesh,
        in_specs=placed,
        out_specs=(P(None, "tile", "pos"), P()),
        check_vma=False,
    )
```

profile of v0, /device:TPU:1, one launch (start us, length us, event | category | flops | bytes accessed | tf_op | source)
XLA Modules:
  0.0 682.2 jit_solution(1483807747958334857)
XLA Ops:
  13.7 22.3 %collective-permute-done = f32[2,512,512]{2,1,0:T(8,128)S(1)} collective-permute-done((f32[2,512,512]{2,1,0:T(8,128)}, f32[2,512,512]{2,1,0:T(8,128)S(1)}, u32[]{:S(2)}, u32[]{:S(2)}) %collective-permute-start) | collective-permute-done | bytes 2097184 | tf_op jit(solution)/shard_map/ppermute | solution.py:12
  42.0 69.3 %collective-permute-done.1 = f32[2,512,1024]{2,1,0:T(8,128)} collective-permute-done((f32[2,512,1024]{2,1,0:T(8,128)}, f32[2,512,1024]{2,1,0:T(8,128)}, u32[]{:S(2)}, u32[]{:S(2)}) %collective-permute-start.1) | collective-permute-done | bytes 4194336 | tf_op jit(solution)/shard_map/ppermute | solution.py:12
  111.4 8.4 %pad_maximum_fusion.20 = f32[2,1024,1024]{2,1,0:T(8,128)} fusion(f32[2,512,1024]{2,1,0:T(8,128)} %collective-permute-done.1, f32[2,512,1024]{2,1,0:T(8,128)} %constant_dynamic-update-slice_fusion), kind=kLoop, calls=%fused_computation.79 | loop fusion | flops 2097152 | bytes 16777216 | tf_op jit(solution)/shard_map/concatenate | solution.py:106
  123.2 16.6 %while.36 = (s32[]{:T(128)}, f32[2,1024,1024]{2,1,0:T(8,128)}, s32[3,3]{1,0:T(4,128)S(1)}, f32[3,2,512,512]{3,2,1,0:T(8,128)}, s32[]{:T(128)}) while((s32[]{:T(128)}, f32[2,1024,1024]{2,1,0:T(8,128)}, s32[3,3]{1,0:T(4,128)S(1)}, f32[3,2,512,512]{3,2,1,0:T(8,128)}, s32[]{:T(128)}) %tuple.127), condition=%wide.while_cond.3, body=%wide.while_body.3.sunk | while | flops 2 | bytes 4195945 | solution.py:115
  123.8 4.9 bitcast_dynamic-update-slice_fusion.2
  129.3 4.9 bitcast_dynamic-update-slice_fusion.2
  134.9 4.9 bitcast_dynamic-update-slice_fusion.2
  139.8 3.5 broadcast_in_dim.7
  144.9 178.8 %while.37 = (s32[]{:T(128)}, f32[3,2,512,512]{3,2,1,0:T(8,128)}, f32[2,512,512]{2,1,0:T(8,128)}, s32[]{:T(128)}, f32[2,512,512]{2,1,0:T(8,128)}, /*index=5*/f32[...) while((s32[]{:T(128)}, f32[3,2,512,512]{3,2,1,0:T(8,128)}, ...), condition=%wide.region_4.5_spmd.clone.clone, body=%wide.region_0.4_spmd.clone.clone.sunk | while | flops 25789726720 | bytes 152045104 | solution.py:95
  168.6 49.5 %conditional.4 = ((f32[3,2,512,512]{3,2,1,0:T(8,128)}, f32[2,512,512]{2,1,0:T(8,128)})) conditional(s32[]{:T(128)} %convert_element_type.41, (f32[3,2,512,512]{3,2,1,0:T(8,128)}, f32[2,512,512]{2,1,0:T(8,128)}) %tuple.123, (s32[]{:T(128)}, f32[2,512,512]{2,1,0:T(8,128)}, f32[3,2,512,512]{3,2,1,0:T(8,128)}, f32[512,512]{1,0:T(8,128)S(1)}, ...), branch_computations={%region_1.1_spmd, %region_2.3_spmd.clone} | conditional | flops 25786056704 | bytes 149947744 | solution.py:92
  171.3 6.8 sine_multiply_fusion
  178.1 3.6 fusion.14
  181.6 3.6 fusion.15
  185.7 3.6 fusion.11
  189.3 3.6 fusion.10
  194.7 3.6 fusion.16
  198.3 3.6 fusion.17
  202.4 3.5 fusion.7
  205.9 3.5 fusion.6
  214.1 4.0 fusion.5
  219.4 49.5 %conditional.4 = ((f32[3,2,512,512]{3,2,1,0:T(8,128)}, f32[2,512,512]{2,1,0:T(8,128)})) conditional(s32[]{:T(128)} %convert_element_type.41, (f32[3,2,512,512]{3,2,1,0:T(8,128)}, f32[2,512,512]{2,1,0:T(8,128)}) %tuple.123, (s32[]{:T(128)}, f32[2,512,512]{2,1,0:T(8,128)}, f32[3,2,512,512]{3,2,1,0:T(8,128)}, f32[512,512]{1,0:T(8,128)S(1)}, ...), branch_computations={%region_1.1_spmd, %region_2.3_spmd.clone} | conditional | flops 25786056704 | bytes 149947744 | solution.py:92
  222.1 6.8 sine_multiply_fusion
  228.9 3.6 fusion.14
  232.4 3.6 fusion.15
  236.5 3.6 fusion.11
  240.1 3.6 fusion.10
  245.5 3.6 fusion.16
  249.1 3.6 fusion.17
  253.2 3.5 fusion.7
  264.9 4.0 fusion.5
  270.2 49.4 %conditional.4 = ((f32[3,2,512,512]{3,2,1,0:T(8,128)}, f32[2,512,512]{2,1,0:T(8,128)})) conditional(s32[]{:T(128)} %convert_element_type.41, (f32[3,2,512,512]{3,2,1,0:T(8,128)}, f32[2,512,512]{2,1,0:T(8,128)}) %tuple.123, (s32[]{:T(128)}, f32[2,512,512]{2,1,0:T(8,128)}, f32[3,2,512,512]{3,2,1,0:T(8,128)}, f32[512,512]{1,0:T(8,128)S(1)}, ...), branch_computations={%region_1.1_spmd, %region_2.3_spmd.clone} | conditional | flops 25786056704 | bytes 149947744 | solution.py:92
  272.9 6.8 sine_multiply_fusion
  279.7 3.6 fusion.14
  283.3 3.6 fusion.15
  287.3 3.6 fusion.11
  290.9 3.6 fusion.10
  296.4 3.6 fusion.16
  299.9 3.6 fusion.17
  307.5 3.5 fusion.6
  315.7 4.0 fusion.5
  323.7 4.3 broadcast_in_dim.6
  328.0 64.5 %while.35 = (s32[]{:T(128)}, f32[2,1024,1024]{2,1,0:T(8,128)}, s32[3,2]{0,1:T(2,128)S(1)}, f32[3,2,512,512]{3,2,1,0:T(8,128)}, s32[]{:T(128)}, /*index=5*/s32[]{:T(128)}, s32[]{:T(128)}) while((s32[]{:T(128)}, f32[2,1024,1024]{2,1,0:T(8,128)}, s32[3,2]{0,1:T(2,128)S(1)}, f32[3,2,512,512]{3,2,1,0:T(8,128)}, s32[]{:T(128)}, ...), condition=%wide.region_6.7_spmd, body=%wide.region_5.6_spmd.sunk | while | flops 524296 | bytes 10485957 | solution.py:138
  335.3 14.4 %dynamic_update_slice.8 = f32[2,1024,1024]{2,1,0:T(8,128)} dynamic-update-slice(f32[2,1024,1024]{2,1,0:T(8,128)} %get-tuple-element.646, f32[2,512,512]{2,1,0:T(8,128)S(1)} %bitcast_add_fusion.2, s32[]{:T(128)} %constant.155.clone.1..sunk, s32[]{:T(128)S(6)} %select_n.84, s32[]{:T(128)S(6)} %select_n.85) | dynamic-update-slice | bytes 4194308 | tf_op jit(solution)/shard_map/while/body/eval_jaxpr/dynamic_update_slice | solution.py:136
  357.0 14.2 %dynamic_update_slice.8 = f32[2,1024,1024]{2,1,0:T(8,128)} dynamic-update-slice(f32[2,1024,1024]{2,1,0:T(8,128)} %get-tuple-element.646, f32[2,512,512]{2,1,0:T(8,128)S(1)} %bitcast_add_fusion.2, s32[]{:T(128)} %constant.155.clone.1..sunk, s32[]{:T(128)S(6)} %select_n.84, s32[]{:T(128)S(6)} %select_n.85) | dynamic-update-slice | bytes 4194308 | tf_op jit(solution)/shard_map/while/body/eval_jaxpr/dynamic_update_slice | solution.py:136
  378.5 14.1 %dynamic_update_slice.8 = f32[2,1024,1024]{2,1,0:T(8,128)} dynamic-update-slice(f32[2,1024,1024]{2,1,0:T(8,128)} %get-tuple-element.646, f32[2,512,512]{2,1,0:T(8,128)S(1)} %bitcast_add_fusion.2, s32[]{:T(128)} %constant.155.clone.1..sunk, s32[]{:T(128)S(6)} %select_n.84, s32[]{:T(128)S(6)} %select_n.85) | dynamic-update-slice | bytes 4194308 | tf_op jit(solution)/shard_map/while/body/eval_jaxpr/dynamic_update_slice | solution.py:136
  397.0 45.2 %collective-permute-done.2 = f32[2,512,1024]{2,1,0:T(8,128)S(1)} collective-permute-done((f32[2,512,1024]{2,1,0:T(8,128)S(1)}, f32[2,512,1024]{2,1,0:T(8,128)S(1)}, u32[]{:S(2)}, u32[]{:S(2)}) %collective-permute-start.2) | collective-permute-done | bytes 4194336 | tf_op jit(solution)/shard_map/ppermute | solution.py:12
  446.1 65.9 %collective-permute-start.3 = (f32[2,512,512]{2,1,0:T(8,128)}, f32[2,512,512]{2,1,0:T(8,128)S(1)}, u32[]{:S(2)}, u32[]{:S(2)}) collective-permute-start(f32[2,512,512]{2,1,0:T(8,128)} %slice.226), channel_id=1, source_target_pairs={{0,1},{1,2},{2,3},{3,4},{4,5},{5,6},{6,7},{7,8},{8,9},{9,10},{10,1... | collective-permute-start | bytes 6291464 | tf_op jit(solution)/shard_map/ppermute | solution.py:12
  512.0 158.1 %all-reduce.2.cloned.1.call-done = f32[2,512,512]{2,1,0:T(8,128)} async-done(((f32[2,512,512]{2,1,0:T(8,128)}), f32[2,512,512]{2,1,0:T(8,128)}) %all-reduce.2.cloned.1.call-update) | async-done | bytes 2097168 | tf_op jit(solution)/shard_map/psum | solution.py:143
  (123 shorter events, 82.8 us)
Async XLA Ops:
  7.2 34.2 %copy-start = (s32[1,16]{1,0:T(1,128)S(1)}, s32[1,16]{1,0:T(1,128)}, u32[]{:S(2)}) copy-start(s32[1,16]{1,0:T(1,128)} %param.22) | copy-start | bytes 196
  7.2 662.9 %all-reduce.2.cloned.1.call-start = ((), (), s32[]{:S(2)}) async-start(), calls=%async_computation | async-start | bytes 4194304 | tf_op jit(solution)/shard_map/psum | solution.py:143
  7.2 28.8 %collective-permute-start = (f32[2,512,512]{2,1,0:T(8,128)}, f32[2,512,512]{2,1,0:T(8,128)S(1)}, u32[]{:S(2)}, u32[]{:S(2)}) collective-permute-start(f32[2,512,512]{2,1,0:T(8,128)} %param.19), channel_id=1, source_target_pairs={{1,0},{2,1},{3,2},{4,3},{5,4},{6,5},{7,6},{8,7},{9,8},{10,9},{11,1... | collective-permute-start | bytes 6291464 | tf_op jit(solution)/shard_map/ppermute | solution.py:12
  13.7 25.1 %copy-start.9 = (s32[1,1,3,2]{2,3,1,0:T(2,128)S(1)}, s32[1,1,3,2]{2,3,1,0:T(2,128)}, u32[]{:S(2)}) copy-start(s32[1,1,3,2]{2,3,1,0:T(2,128)} %param.21) | copy-start | bytes 76
  13.7 25.3 %copy-start.8 = (f32[1,1,3,512,512]{4,3,2,1,0:T(8,128)S(1)}, f32[1,1,3,512,512]{4,3,2,1,0:T(8,128)}, u32[]{:S(2)}) copy-start(f32[1,1,3,512,512]{4,3,2,1,0:T(8,128)} %param.23) | copy-start | bytes 9437188
  37.6 73.8 %collective-permute-start.1 = (f32[2,512,1024]{2,1,0:T(8,128)}, f32[2,512,1024]{2,1,0:T(8,128)}, u32[]{:S(2)}, u32[]{:S(2)}) collective-permute-start(f32[2,512,1024]{2,1,0:T(8,128)} %constant_dynamic-update-slice_fusion), channel_id=1, source_target_pairs={{16,0},{32,16},{48,32},{64,48},{80,64},{96,80},{112,96},{17,1},{33... | collective-permute-start | bytes 12582920 | tf_op jit(solution)/shard_map/ppermute | solution.py:12
  201.9 7.5 %slice-start = ((s8[6291456]{0:T(1024)(128)(4,1)}), s8[4194304]{0:T(1024)(128)(4,1)S(1)}, s32[]{:S(2)}) async-start(s8[6291456]{0:T(1024)(128)(4,1)} %bitcast.125), calls=%async_computation.1 | async-start | bytes 8388608 | tf_op jit(solution)/shard_map/while/body/eval_jaxpr/cond
  202.4 7.0 %slice-start.1 = ((s8[6291456]{0:T(1024)(128)(4,1)}), s8[2097152]{0:T(1024)(128)(4,1)S(1)}, s32[]{:S(2)}) async-start(s8[6291456]{0:T(1024)(128)(4,1)} %bitcast.125), calls=%async_computation.2 | async-start | bytes 4194304 | tf_op jit(solution)/shard_map/while/body/eval_jaxpr/cond
  209.4 1.6 copy-start.2
  210.9 1.6 copy-start.3
  212.5 0.7 copy-start.11
  213.1 5.0 copy-start.4
  252.7 7.5 %slice-start = ((s8[6291456]{0:T(1024)(128)(4,1)}), s8[4194304]{0:T(1024)(128)(4,1)S(1)}, s32[]{:S(2)}) async-start(s8[6291456]{0:T(1024)(128)(4,1)} %bitcast.125), calls=%async_computation.1 | async-start | bytes 8388608 | tf_op jit(solution)/shard_map/while/body/eval_jaxpr/cond
  253.2 7.0 %slice-start.1 = ((s8[6291456]{0:T(1024)(128)(4,1)}), s8[2097152]{0:T(1024)(128)(4,1)S(1)}, s32[]{:S(2)}) async-start(s8[6291456]{0:T(1024)(128)(4,1)} %bitcast.125), calls=%async_computation.2 | async-start | bytes 4194304 | tf_op jit(solution)/shard_map/while/body/eval_jaxpr/cond
  260.2 1.6 copy-start.2
  261.8 1.6 copy-start.3
  263.3 0.7 copy-start.11
  263.9 5.0 copy-start.4
  303.5 7.5 %slice-start = ((s8[6291456]{0:T(1024)(128)(4,1)}), s8[4194304]{0:T(1024)(128)(4,1)S(1)}, s32[]{:S(2)}) async-start(s8[6291456]{0:T(1024)(128)(4,1)} %bitcast.125), calls=%async_computation.1 | async-start | bytes 8388608 | tf_op jit(solution)/shard_map/while/body/eval_jaxpr/cond
  304.0 7.0 %slice-start.1 = ((s8[6291456]{0:T(1024)(128)(4,1)}), s8[2097152]{0:T(1024)(128)(4,1)S(1)}, s32[]{:S(2)}) async-start(s8[6291456]{0:T(1024)(128)(4,1)} %bitcast.125), calls=%async_computation.2 | async-start | bytes 4194304 | tf_op jit(solution)/shard_map/while/body/eval_jaxpr/cond
  311.0 1.6 copy-start.2
  312.6 1.6 copy-start.3
  314.2 0.7 copy-start.11
  314.7 4.9 copy-start.4
  323.7 4.4 copy-start.10
  392.5 49.7 %copy-start.5 = (f32[2,1024,1024]{2,1,0:T(8,128)S(1)}, f32[2,1024,1024]{2,1,0:T(8,128)}, u32[]{:S(2)}) copy-start(f32[2,1024,1024]{2,1,0:T(8,128)} %get-tuple-element.345) | copy-start | bytes 25165828
  395.2 47.0 %collective-permute-start.2 = (f32[2,512,1024]{2,1,0:T(8,128)S(1)}, f32[2,512,1024]{2,1,0:T(8,128)S(1)}, u32[]{:S(2)}, u32[]{:S(2)}) collective-permute-start(f32[2,512,1024]{2,1,0:T(8,128)S(1)} %slice.171), channel_id=1, source_target_pairs={{0,16},{16,32},{32,48},{48,64},{64,80},{80,96},{96,112},{1,17},{17... | collective-permute-start | bytes 12582920 | tf_op jit(solution)/shard_map/ppermute | solution.py:12
  443.6 2.6 copy-start.6
  446.1 227.3 %collective-permute-start.3 = (f32[2,512,512]{2,1,0:T(8,128)}, f32[2,512,512]{2,1,0:T(8,128)S(1)}, u32[]{:S(2)}, u32[]{:S(2)}) collective-permute-start(f32[2,512,512]{2,1,0:T(8,128)} %slice.226), channel_id=1, source_target_pairs={{0,1},{1,2},{2,3},{3,4},{4,5},{5,6},{6,7},{7,8},{8,9},{9,10},{10,1... | collective-permute-start | bytes 6291464 | tf_op jit(solution)/shard_map/ppermute | solution.py:12
  670.1 3.3 copy-start.7
  670.1 5.1 copy-start.1
Sparse Core Ops, SparseCore 0:
  512.1 157.8 all-reduce.1
where the time goes:
time: 688 us; the launch traced here: 682 us
  waiting for transfers between devices  295 us (43%)
  local copies, waits for them, and re-layouts  91.7 us (13%)
  matrix products  85.3 us (12%)
  other arithmetic  83.7 us (12%)
  starting transfers between devices  72.3 us (11%)
  loops' own time  40 us (6%)
  between operations  14.3 us (2%)
    psum x1, waiting for transfers between devices, on_device(): probe_total = lax.psum(probe_sum, ('tile', 'pos'))  158 us
    ppermute x4, waiting for transfers between devices, passed_along(): return lax.ppermute(x, axis, pairs)  137 us
    dot_general x24, matrix products, matmul(): jnp.dot(left_op, right_op, precision=lax.Precision.HIGHEST, preferred_ele...  85.3 us
    ppermute x4, starting transfers between devices, passed_along(): return lax.ppermute(x, axis, pairs)  72.3 us
    dynamic_update_slice x3, local copies, waits for them, and re-layouts, place_term(): lax.dynamic_update_slice(grad_buffer, current + own_terms[slot], corner)  42.7 us
    another operation x1, loops' own time, run_items(): return lax.fori_loop(0, step_count, one_item, start_state)  28.6 us
    mul x3, other arithmetic, dft_tables(): return (jnp.cos(angles) * factor, jnp.sin(angles) * factor)  20.3 us
    gather x9, local copies, waits for them, and re-layouts  16.6 us
  transfers between devices with their start and end apart: 5, of which 4 were waited for; matrix products, arithmetic and copies ran while one was open for 1% of the time, Pallas kernels for 0%

commit v1 on v0

v1 whole, which is shorter than its diff:
```python
import functools
import math

import jax
import jax.numpy as jnp
import numpy as np
from jax import lax
from jax.experimental import pallas as pl
from jax.experimental.pallas import tpu as pltpu
from jax.sharding import PartitionSpec as P

MESH = pl.DeviceIdType.MESH
WIN = 512
SLOTS = 3
ROWS = 64
CHUNKS = WIN // ROWS
LAG = 2
TILES = 8
COLS = 16
SEAM = 8
QUARTER = WIN // 4
SLAB = 256
RIGHT, LOWER, CORNER = 0, 1, 2
F32 = jnp.float32
BF16 = jnp.bfloat16


def split_table(table):
    high = table.astype(BF16)
    low = (table - high.astype(np.float64)).astype(BF16)
    return high, low


def row_tables():
    points = np.arange(WIN)
    angles = (points[:, None] * points[None, :] % WIN) * (2.0 * math.pi / WIN)
    stacked = np.concatenate([np.cos(angles), np.sin(angles)], axis=0) / math.sqrt(WIN)
    return split_table(stacked)


def column_tables():
    blocks = []
    for residue in range(4):
        freqs = 4 * np.arange(QUARTER) + residue
        angles = (freqs[:, None] * np.arange(QUARTER)[None, :] % WIN) * (2.0 * math.pi / WIN)
        cosine = np.cos(angles) / math.sqrt(WIN)
        sine = np.sin(angles) / math.sqrt(WIN)
        blocks.append(np.block([[cosine, sine], [-sine, cosine]]))
    forward = np.stack(blocks)
    backward = np.swapaxes(forward, 1, 2)
    return split_table(np.stack([forward, backward]))


def split_value(value):
    high = value.astype(BF16)
    low = (value - high.astype(F32)).astype(BF16)
    return high, low


def dot(left, right):
    return jnp.dot(left, right, preferred_element_type=F32)


def one_hot(shape, axis, base, amount):
    along = lax.broadcasted_iota(jnp.int32, shape, axis)
    other = lax.broadcasted_iota(jnp.int32, shape, 1 - axis)
    return jnp.where(along == ((other + (base + amount)) & (WIN - 1)), 1.0, 0.0).astype(BF16)


def chunk_rows(k):
    return pl.ds(pl.multiple_of(k * ROWS, ROWS), ROWS)


def device_at(z, y, x, core):
    return (z * 2 + y % 2, ((y // 2) * 4 + x) * 2 + core)


def kernel(
    place, counts, obj, probe, inten, row_hi, row_lo, col_hi, col_lo,
    out_obj, out_probe,
    own, halo, grad, back, spec, turned, term_hi, term_lo, roll_cols, unroll_cols, measured,
    wh, wl, ch, cl, left_hi, left_lo,
    probe_sum, pair_in, z_in, plane_in, gathered,
    load_sem, out_sem,
    up_s, up_r, side_s, side_r, cor_s, cor_r,
    gb_s, gb_r, gc_s, gc_r, gd_s, gd_r,
    pair_s, pair_r, z_s, z_r, plane_s, plane_r, ag_s, ag_r, zg_s, zg_r, pg_s, pg_r,
):
    t = lax.axis_index("tile")
    p = lax.axis_index("pos")
    z = t // 2
    core = p % 2
    x = (p // 2) % 4
    y = (p // 8) * 2 + t % 2
    plane_me = y * 4 + x
    own_count = counts[p]
    partner = (t, p + 1 - 2 * core)

    loads = [
        pltpu.make_async_copy(obj, own, load_sem.at[0]),
        pltpu.make_async_copy(probe, probe_sum, load_sem.at[1]),
        pltpu.make_async_copy(row_hi, wh, load_sem.at[2]),
        pltpu.make_async_copy(row_lo, wl, load_sem.at[3]),
        pltpu.make_async_copy(col_hi, ch, load_sem.at[4]),
        pltpu.make_async_copy(col_lo, cl, load_sem.at[5]),
    ]
    for lanes in range(4):
        loads.append(
            pltpu.make_async_copy(
                inten.at[:, :, pl.ds(lanes * QUARTER, QUARTER)], measured.at[lanes],
                load_sem.at[6 + lanes],
            )
        )
    for load in loads:
        load.start()

    barrier = pltpu.get_barrier_semaphore()

    def greet(device):
        pl.semaphore_signal(barrier, inc=1, device_id=device, device_id_type=MESH)

    t_up = (t + TILES - 1) % TILES
    t_down = (t + 1) % TILES
    p_left = (p + COLS - 1) % COLS
    p_right = (p + 1) % COLS
    for device in (
        (t_up, p), (t_down, p), (t, p_left), (t, p_right), (t_up, p_left), (t_down, p_right),
    ):
        greet(device)
    for step in range(1, 4):
        greet(device_at((z + step) % 4, y, x, core))

    def greet_plane(step, carry):
        peer = (plane_me + step) % 16
        greet(device_at(z, peer // 4, peer % 4, core))
        return carry

    lax.fori_loop(1, 16, greet_plane, 0)
    pl.semaphore_wait(barrier, 6 + 3 + 15)

    def remote(source, target, send, recv, device):
        return pltpu.make_async_remote_copy(
            src_ref=source, dst_ref=target, send_sem=send, recv_sem=recv,
            device_id=device, device_id_type=MESH,
        )

    def up_copy(k):
        rows = chunk_rows(k)
        return remote(
            obj.at[:, rows, :], halo.at[LOWER, :, rows, :], up_s.at[k], up_r.at[k], (t_up, p)
        )

    def side_copy(k):
        rows = chunk_rows(k)
        return remote(
            obj.at[:, rows, :], halo.at[RIGHT, :, rows, :], side_s.at[k], side_r.at[k], (t, p_left)
        )

    def corner_copy(k):
        rows = chunk_rows(k)
        return remote(
            halo.at[LOWER, :, rows, :], halo.at[CORNER, :, rows, :], cor_s.at[k], cor_r.at[k],
            (t, p_left),
        )

    def corner_direct(k):
        rows = chunk_rows(k)
        return remote(
            obj.at[:, rows, :], halo.at[CORNER, :, rows, :], cor_s.at[k], cor_r.at[k],
            (t_up, p_left),
        )

    def grad_side(k):
        rows = chunk_rows(k)
        return remote(
            grad.at[1, :, rows, :], back.at[RIGHT, :, rows, :], gb_s.at[k], gb_r.at[k],
            (t, p_right),
        )

    def grad_down(k):
        rows = chunk_rows(k)
        return remote(
            grad.at[2, :, rows, :], back.at[LOWER, :, rows, :], gc_s.at[k], gc_r.at[k],
            (t_down, p),
        )

    def grad_corner(k):
        rows = chunk_rows(k)
        return remote(
            grad.at[3, :, rows, :], back.at[CORNER, :, rows, :], gd_s.at[k], gd_r.at[k],
            (t, p_right),
        )

    def grad_corner_direct(k):
        rows = chunk_rows(k)
        return remote(
            grad.at[3, :, rows, :], back.at[CORNER, :, rows, :], gd_s.at[k], gd_r.at[k],
            (t_down, p_right),
        )

    has_up = t > 0
    has_down = t < TILES - 1
    has_left = p > 0
    has_right = p < COLS - 1
    after_seam = p == SEAM
    before_seam = p == SEAM - 1
    passes_on = has_left & has_down & jnp.logical_not(after_seam)

    def first_sends(k, carry):
        @pl.when(has_up)
        def _():
            up_copy(k).start()

        @pl.when(has_left)
        def _():
            side_copy(k).start()

        @pl.when(has_up & after_seam)
        def _():
            corner_direct(k).start()

        return carry

    lax.fori_loop(0, CHUNKS, first_sends, 0)

    for load in loads[:4]:
        load.wait()

    for part in range(2):
        high, low = split_value(probe_sum[part])
        term_hi[pl.ds(0, WIN), pl.ds(part * WIN, WIN)] = high
        term_lo[pl.ds(0, WIN), pl.ds(part * WIN, WIN)] = low

    def build_rolls(s, carry):
        amount = place[2 * s + 1]
        roll_cols[s] = one_hot((WIN, WIN), 1, 0, amount)
        unroll_cols[s] = one_hot((WIN, WIN), 0, 0, amount)
        return carry

    lax.fori_loop(0, SLOTS, build_rolls, 0)

    def roll_probe(step, carry):
        s = step // 4
        base = (step % 4) * QUARTER
        rows = pl.ds(pl.multiple_of(base, QUARTER), QUARTER)
        pick = one_hot((QUARTER, WIN), 1, base, WIN - place[2 * s])
        for part in range(2):
            columns = pl.ds(part * WIN, WIN)
            moved = dot(pick, term_hi[pl.ds(0, WIN), columns])
            moved += dot(pick, term_lo[pl.ds(0, WIN), columns])
            high, low = split_value(moved)
            turned[s, part, rows, :] = dot(high, roll_cols[s]) + dot(low, roll_cols[s])
        return carry

    lax.fori_loop(0, SLOTS * 4, roll_probe, 0)

    row_iota = lax.broadcasted_iota(jnp.int32, (ROWS, WIN), 0)
    col_iota = lax.broadcasted_iota(jnp.int32, (ROWS, WIN), 1)

    def slot_masks(s, k):
        above = (row_iota + k * ROWS) < place[2 * s]
        before = col_iota < place[2 * s + 1]
        return above, before

    def patch_part(part, rows, above, before):
        upper = jnp.where(before, halo[RIGHT, part, rows, :], own[part, rows, :])
        lower = jnp.where(before, halo[CORNER, part, rows, :], halo[LOWER, part, rows, :])
        return jnp.where(above, lower, upper)

    def put_left(s, real, imag, sign):
        top = pl.ds(s * ROWS, ROWS)
        low_rows = pl.ds((SLOTS + s) * ROWS, ROWS)
        first = pl.ds(0, WIN)
        second = pl.ds(WIN, WIN)
        for ref, re, im in zip((left_hi, left_lo), split_value(real), split_value(imag)):
            ref[top, first] = re
            ref[low_rows, first] = im
            if sign > 0:
                ref[top, second] = im
                ref[low_rows, second] = -re
            else:
                ref[top, second] = -im
                ref[low_rows, second] = re

    def row_transform(cols):
        columns = pl.ds(cols * SLAB, SLAB)
        high = left_hi[...]
        table = wh[:, columns]
        total = dot(high, table)
        total = total + dot(left_lo[...], table)
        return total + dot(high, wl[:, columns])

    def forward_chunk(k):
        rows = chunk_rows(k)
        for s in range(SLOTS):
            above, before = slot_masks(s, k)
            re = patch_part(0, rows, above, before)
            im = patch_part(1, rows, above, before)
            pr = turned[s, 0, rows, :]
            pi = turned[s, 1, rows, :]
            put_left(s, pr * re - pi * im, pr * im + pi * re, 1)
        for cols in range(WIN // SLAB):
            total = row_transform(cols)
            for s in range(SLOTS):
                for part in range(2):
                    base = (part * SLOTS + s) * ROWS
                    spec[s, part, rows, pl.ds(cols * SLAB, SLAB)] = total[base:base + ROWS]

    def forward_step(j, carry):
        @pl.when(j < CHUNKS)
        def _():
            @pl.when(has_down)
            def _():
                up_copy(j).wait_recv()

            @pl.when(passes_on)
            def _():
                corner_copy(j).start()

        @pl.when(j >= LAG)
        def _():
            k = j - LAG

            @pl.when(has_right)
            def _():
                side_copy(k).wait_recv()

            @pl.when(has_right & has_down)
            def _():
                corner_copy(k).wait_recv()

            forward_chunk(k)

        return carry

    lax.fori_loop(0, CHUNKS + LAG, forward_step, 0)

    for load in loads[4:]:
        load.wait()

    def middle(step, carry):
        s = step // (WIN // SLAB)
        slab = step % (WIN // SLAB)
        columns = pl.ds(pl.multiple_of(slab * SLAB, SLAB), SLAB)

        def quarter(part, j):
            return spec[s, part, pl.ds(j * QUARTER, QUARTER), columns]

        re = [quarter(0, j) for j in range(4)]
        im = [quarter(1, j) for j in range(4)]
        er, ei = re[0] + re[2], im[0] + im[2]
        fr, fi = re[0] - re[2], im[0] - im[2]
        gr, gi = re[1] + re[3], im[1] + im[3]
        hr, hi = re[1] - re[3], im[1] - im[3]
        mixed = [
            (er + gr, ei + gi), (fr + hi, fi - hr), (er - gr, ei - gi), (fr - hi, fi + hr),
        ]
        outs = []
        for q in range(4):
            high, low = split_value(jnp.concatenate(mixed[q], axis=0))
            total = dot(ch[0, q], high) + dot(cl[0, q], high) + dot(ch[0, q], low)
            sr, si = total[:QUARTER], total[QUARTER:]
            levels = [measured[2 * slab + n, s, pl.ds(q, QUARTER, stride=4), :] for n in range(2)]
            miss = sr * sr + si * si - jnp.concatenate(levels, axis=1)
            high, low = split_value(jnp.concatenate([miss * sr, miss * si], axis=0))
            total = dot(ch[1, q], high) + dot(cl[1, q], high) + dot(ch[1, q], low)
            outs.append((total[:QUARTER], total[QUARTER:]))
        (ar, ai), (br, bi), (cr, ci), (dr, di) = outs
        er, ei = ar + cr, ai + ci
        fr, fi = ar - cr, ai - ci
        gr, gi = br + dr, bi + di
        hr, hi = br - dr, bi - di
        results = [
            (er + gr, ei + gi), (fr - hi, fi + hr), (er - gr, ei - gi), (fr + hi, fi - hr),
        ]
        for j in range(4):
            for part in range(2):
                spec[s, part, pl.ds(j * QUARTER, QUARTER), columns] = results[j][part]
        return carry

    lax.fori_loop(0, SLOTS * (WIN // SLAB), middle, 0)

    def backward_chunk(k):
        rows = chunk_rows(k)
        for s in range(SLOTS):
            put_left(s, spec[s, 0, rows, :], spec[s, 1, rows, :], -1)
        for cols in range(WIN // SLAB):
            total = row_transform(cols)
            for s in range(SLOTS):
                for part in range(2):
                    base = (part * SLOTS + s) * ROWS
                    spec[s, part, rows, pl.ds(cols * SLAB, SLAB)] = total[base:base + ROWS]
        zero = jnp.zeros((ROWS, WIN), F32)
        sums = [[zero, zero] for _ in range(4)]
        for s in range(SLOTS):
            used = own_count > s
            above, before = slot_masks(s, k)
            br = spec[s, 0, rows, :]
            bi = spec[s, 1, rows, :]
            pr = turned[s, 0, rows, :]
            pi = turned[s, 1, rows, :]
            terms = (pr * br + pi * bi, pr * bi - pi * br)
            for part in range(2):
                term = jnp.where(used, terms[part], zero)
                lower = jnp.where(above, term, zero)
                upper = term - lower
                upper_right = jnp.where(before, upper, zero)
                lower_right = jnp.where(before, lower, zero)
                sums[0][part] += upper - upper_right
                sums[1][part] += upper_right
                sums[2][part] += lower - lower_right
                sums[3][part] += lower_right
            re = patch_part(0, rows, above, before)
            im = patch_part(1, rows, above, before)
            terms = (re * br + im * bi, re * bi - im * br)
            high, low = split_value(jnp.where(used, jnp.concatenate(terms, axis=0), 0.0))
            moved = dot(high, unroll_cols[s]) + dot(low, unroll_cols[s])
            high, low = split_value(moved)
            term_rows = pl.ds(pl.multiple_of(s * WIN + k * ROWS, ROWS), ROWS)
            for part in range(2):
                columns = pl.ds(part * WIN, WIN)
                term_hi[term_rows, columns] = high[part * ROWS:(part + 1) * ROWS]
                term_lo[term_rows, columns] = low[part * ROWS:(part + 1) * ROWS]
        for block in range(4):
            for part in range(2):
                grad[block, part, rows, :] = sums[block][part]

    receives_corner = has_left & jnp.logical_not(after_seam) & has_down

    def add_down(k):
        rows = chunk_rows(k)

        @pl.when(receives_corner)
        def _():
            grad_corner(k).wait_recv()
            for part in range(2):
                grad[2, part, rows, :] += back[CORNER, part, rows, :]

        @pl.when(has_down)
        def _():
            grad_down(k).start()

    def backward_step(j, carry):
        @pl.when(j < CHUNKS)
        def _():
            backward_chunk(j)

            @pl.when(has_right & has_down & jnp.logical_not(before_seam))
            def _():
                grad_corner(j).start()

            @pl.when(has_down & before_seam)
            def _():
                grad_corner_direct(j).start()

        @pl.when(j >= LAG)
        def _():
            k = j - LAG
            add_down(k)

            @pl.when(has_right)
            def _():
                grad_side(k).start()

        return carry

    lax.fori_loop(0, CHUNKS + LAG, backward_step, 0)

    def unroll_term(step, carry):
        base = step * QUARTER
        rows = pl.ds(pl.multiple_of(base, QUARTER), QUARTER)
        picks = [one_hot((QUARTER, WIN), 1, base, place[2 * s]) for s in range(SLOTS)]
        pick = jnp.concatenate(picks, axis=1)
        for part in range(2):
            columns = pl.ds(part * WIN, WIN)
            probe_sum[part, rows, :] = dot(pick, term_hi[:, columns]) + dot(pick, term_lo[:, columns])
        return carry

    lax.fori_loop(0, 4, unroll_term, 0)

    half = WIN // 2
    mine = pl.multiple_of(core * half, half)
    theirs = pl.multiple_of((1 - core) * half, half)
    pair_copy = remote(
        probe_sum.at[:, pl.ds(theirs, half), :], pair_in, pair_s, pair_r, partner
    )
    pair_copy.start()
    pair_copy.wait_recv()

    def add_pair(k, carry):
        for part in range(2):
            rows = pl.ds(pl.multiple_of(mine + k * ROWS, ROWS), ROWS)
            probe_sum[part, rows, :] += pair_in[part, chunk_rows(k), :]
        return carry

    lax.fori_loop(0, half // ROWS, add_pair, 0)

    def z_copy(step):
        peer = (z + step) % 4
        rows = pl.ds(pl.multiple_of(mine + peer * ROWS, ROWS), ROWS)
        return remote(
            probe_sum.at[:, rows, :], z_in.at[step - 1], z_s.at[step - 1], z_r.at[step - 1],
            device_at(peer, y, x, core),
        )

    for step in (2, 1, 3):
        z_copy(step).start()
    z_rows = pl.ds(pl.multiple_of(mine + z * ROWS, ROWS), ROWS)
    for step in (1, 2, 3):
        z_copy(step).wait_recv()
    for part in range(2):
        probe_sum[part, z_rows, :] += z_in[0, part] + z_in[1, part] + z_in[2, part]

    def piece(index):
        return index // 8, pl.ds(pl.multiple_of(mine + z * ROWS + (index % 8) * 8, 8), 8)

    def plane_copy(step):
        peer = (plane_me + step) % 16
        part, rows = piece(peer)
        return remote(
            probe_sum.at[part, rows, :], plane_in.at[step - 1], plane_s.at[step - 1],
            plane_r.at[step - 1], device_at(z, peer // 4, peer % 4, core),
        )

    def start_plane(step, carry):
        plane_copy(step).start()
        return carry

    lax.fori_loop(1, 16, start_plane, 0)
    my_part, my_rows = piece(plane_me)

    def add_plane(step, total):
        plane_copy(step).wait_recv()
        return total + plane_in[step - 1]

    total = lax.fori_loop(1, 16, add_plane, probe_sum[my_part, my_rows, :])
    gathered[my_part, my_rows, :] = total * (1.0 / (TILES * COLS * SLOTS))

    def gather_copy(step):
        peer = (plane_me + step) % 16
        return remote(
            gathered.at[my_part, my_rows, :], gathered.at[my_part, my_rows, :],
            ag_s.at[step - 1], ag_r.at[step - 1], device_at(z, peer // 4, peer % 4, core),
        )

    def start_gather(step, carry):
        gather_copy(step).start()
        return carry

    def wait_gather(step, carry):
        gather_copy(step).wait_recv()
        return carry

    lax.fori_loop(1, 16, start_gather, 0)
    lax.fori_loop(1, 16, wait_gather, 0)

    def z_gather(step):
        peer = (z + step) % 4
        return remote(
            gathered.at[:, z_rows, :], gathered.at[:, z_rows, :], zg_s.at[step - 1],
            zg_r.at[step - 1], device_at(peer, y, x, core),
        )

    for step in (2, 1, 3):
        z_gather(step).start()
    for step in (1, 2, 3):
        z_gather(step).wait_recv()
    pair_gather = remote(
        gathered.at[:, pl.ds(mine, half), :], gathered.at[:, pl.ds(mine, half), :], pg_s, pg_r,
        partner,
    )
    pair_gather.start()

    def out_copy(k):
        rows = chunk_rows(k)
        return pltpu.make_async_copy(
            grad.at[0, :, rows, :], out_obj.at[:, rows, :], out_sem.at[k]
        )

    def finish(k, carry):
        rows = chunk_rows(k)

        @pl.when(has_left)
        def _():
            grad_side(k).wait_recv()
            for part in range(2):
                grad[0, part, rows, :] += back[RIGHT, part, rows, :]

        @pl.when(after_seam & has_up)
        def _():
            grad_corner(k).wait_recv()
            for part in range(2):
                grad[0, part, rows, :] += back[CORNER, part, rows, :]

        @pl.when(has_up)
        def _():
            grad_down(k).wait_recv()
            for part in range(2):
                grad[0, part, rows, :] += back[LOWER, part, rows, :]

        out_copy(k).start()
        return carry

    lax.fori_loop(0, CHUNKS, finish, 0)
    pair_gather.wait_recv()
    probe_out = pltpu.make_async_copy(gathered, out_probe, out_sem.at[CHUNKS])
    probe_out.start()

    def drain(k, carry):
        @pl.when(has_up)
        def _():
            up_copy(k).wait_send()

        @pl.when(has_left)
        def _():
            side_copy(k).wait_send()

        @pl.when(passes_on | (has_up & after_seam))
        def _():
            corner_copy(k).wait_send()

        @pl.when(has_right)
        def _():
            grad_side(k).wait_send()

        @pl.when(has_down)
        def _():
            grad_down(k).wait_send()

        @pl.when(has_right & has_down)
        def _():
            grad_corner(k).wait_send()

        out_copy(k).wait()
        return carry

    lax.fori_loop(0, CHUNKS, drain, 0)

    def drain_plane(step, carry):
        plane_copy(step).wait_send()
        gather_copy(step).wait_send()
        return carry

    lax.fori_loop(1, 16, drain_plane, 0)
    for step in (1, 2, 3):
        z_copy(step).wait_send()
        z_gather(step).wait_send()
    pair_copy.wait_send()
    pair_gather.wait_send()
    probe_out.wait()


def on_device(object_field, probe_field, offsets, counts, intensity):
    place = offsets.reshape(2 * SLOTS)
    count_row = counts.reshape(COLS)
    measured = intensity.reshape(SLOTS, WIN, WIN)
    row_hi, row_lo = row_tables()
    col_hi, col_lo = column_tables()
    block = (2, WIN, WIN)
    dma = pltpu.SemaphoreType.DMA
    anywhere = pl.BlockSpec(memory_space=pl.ANY)
    scalars = pl.BlockSpec(memory_space=pltpu.SMEM)
    return pl.pallas_call(
        kernel,
        name="ptycho_step",
        out_shape=(jax.ShapeDtypeStruct(block, F32), jax.ShapeDtypeStruct(block, F32)),
        in_specs=[scalars, scalars] + [anywhere] * 7,
        out_specs=(anywhere, anywhere),
        scratch_shapes=[
            pltpu.VMEM(block, F32),
            pltpu.VMEM((3,) + block, F32),
            pltpu.VMEM((4,) + block, F32),
            pltpu.VMEM((3,) + block, F32),
            pltpu.VMEM((SLOTS,) + block, F32),
            pltpu.VMEM((SLOTS,) + block, F32),
            pltpu.VMEM((SLOTS * WIN, 2 * WIN), BF16),
            pltpu.VMEM((SLOTS * WIN, 2 * WIN), BF16),
            pltpu.VMEM((SLOTS, WIN, WIN), BF16),
            pltpu.VMEM((SLOTS, WIN, WIN), BF16),
            pltpu.VMEM((4, SLOTS, WIN, QUARTER), F32),
            pltpu.VMEM((2 * WIN, WIN), BF16),
            pltpu.VMEM((2 * WIN, WIN), BF16),
            pltpu.VMEM((2, 4, 2 * QUARTER, 2 * QUARTER), BF16),
            pltpu.VMEM((2, 4, 2 * QUARTER, 2 * QUARTER), BF16),
            pltpu.VMEM((2 * SLOTS * ROWS, 2 * WIN), BF16),
            pltpu.VMEM((2 * SLOTS * ROWS, 2 * WIN), BF16),
            pltpu.VMEM(block, F32),
            pltpu.VMEM((2, WIN // 2, WIN), F32),
            pltpu.VMEM((3, 2, ROWS, WIN), F32),
            pltpu.VMEM((15, 8, WIN), F32),
            pltpu.VMEM(block, F32),
            dma((10,)), dma((CHUNKS + 1,)),
            dma((CHUNKS,)), dma((CHUNKS,)), dma((CHUNKS,)), dma((CHUNKS,)),
            dma((CHUNKS,)), dma((CHUNKS,)), dma((CHUNKS,)), dma((CHUNKS,)),
            dma((CHUNKS,)), dma((CHUNKS,)), dma((CHUNKS,)), dma((CHUNKS,)),
            dma, dma, dma((3,)), dma((3,)), dma((15,)), dma((15,)),
            dma((15,)), dma((15,)), dma((3,)), dma((3,)), dma, dma,
        ],
        compiler_params=pltpu.CompilerParams(
            collective_id=0, has_side_effects=True, vmem_limit_bytes=62 * 1024 * 1024
        ),
        cost_estimate=pl.CostEstimate(
            flops=20_000_000_000, bytes_accessed=16_000_000, transcendentals=0
        ),
    )(
        place, count_row, object_field, probe_field, measured,
        jnp.asarray(row_hi), jnp.asarray(row_lo), jnp.asarray(col_hi), jnp.asarray(col_lo),
    )


def solution(mesh):
    placed = (
        P(None, "tile", "pos"),
        P(),
        P("tile", "pos", None, None),
        P("tile", None),
        P("tile", "pos", None, None, None),
    )
    return jax.shard_map(
        on_device,
        mesh=mesh,
        in_specs=placed,
        out_specs=(P(None, "tile", "pos"), P()),
        check_vma=False,
    )
```

time: 688 us -> 194 us (0.28)
  waiting for transfers between devices: 295 us -> 0 us
  Pallas kernels: 0 us -> 187 us
  local copies, waits for them, and re-layouts: 91.7 us -> 5.91 us
  matrix products: 85.3 us -> 0 us
  other arithmetic: 83.7 us -> 0 us
  starting transfers between devices: 72.3 us -> 0 us
  loops' own time: 40 us -> 0 us
  between operations: 14.3 us -> 0.65 us
    pallas_call x0 -> x1, Pallas kernels: none -> 187 us  [on_device(): pl.pallas_call(kernel, name='ptycho_step', out_shape=(jax.ShapeDtypeStruc...]
    psum x1 -> x0, waiting for transfers between devices: 158 us -> none  [on_device(): probe_total = lax.psum(probe_sum, ('tile', 'pos'))]
    ppermute x4 -> x0, waiting for transfers between devices: 137 us -> none  [passed_along(): return lax.ppermute(x, axis, pairs)]
    dot_general x24 -> x0, matrix products: 85.3 us -> none  [matmul(): jnp.dot(left_op, right_op, precision=lax.Precision.HIGHEST, preferred_ele...]
    ppermute x4 -> x0, starting transfers between devices: 72.3 us -> none  [passed_along(): return lax.ppermute(x, axis, pairs)]
    dynamic_update_slice x3 -> x0, local copies, waits for them, and re-layouts: 42.7 us -> none  [place_term(): lax.dynamic_update_slice(grad_buffer, current + own_terms[slot], corner)]
    another operation x6 -> x0, loops' own time: 40 us -> none  [the longest x1 28.6 us: run_items(): return lax.fori_loop(0, step_count, one_item, start_state)]
    mul x10 -> x0, other arithmetic: 30.4 us -> none  [the longest x3 20.3 us: dft_tables(): return (jnp.cos(angles) * factor, jnp.sin(angles) * factor)]
  transfers between devices with their start and end apart: 5 -> 0, of which waited for: 4 -> 0; matrix products, arithmetic and copies ran while one was open for 1% -> 0% of each run, Pallas kernels for 0% -> 0%
where the time goes in v1:
time: 194 us
  Pallas kernels  187 us (96%)
  local copies, waits for them, and re-layouts  5.91 us (3%)
    pallas_call x1, Pallas kernels, on_device(): pl.pallas_call(kernel, name='ptycho_step', out_shape=(jax.ShapeDtypeStruc...  187 us
    unnamed x5, local copies, waits for them, and re-layouts  5.32 us

profile of v1, /device:TPU:1, one launch (start us, length us, event | category | flops | bytes accessed | tf_op | source)
XLA Modules:
  0.0 194.0 jit_solution(9684654701580199594)
XLA Ops:
  0.6 0.8 copy.12
  1.4 0.6 reshape.13.place
  2.0 187.5 %ptycho_step.1 = (f32[2,512,512]{2,1,0:T(8,128)}, f32[2,512,512]{2,1,0:T(8,128)}) custom-call(s32[6]{0:T(128)} %reshape.13.place, s32[16]{0:T(128)} %bitcast.3, f32[2,512,512]{2,1,0:T(8,128)} %obj.1, f32[2,512,512]{2,1,0:T(8,128)} %probe.1, f32[3,512,512]{2,1,0:T(8,128)} %bitcast.2, bf16[1024,512]{1,0:T(8,128)(2,1)} %constant.8.clone.row_hi, ...), custom_call_target="tpu_custom_call" | custom-call | flops 20000000000 | bytes 16000000 | tf_op jit(solution)/shard_map/ptycho_step/pallas_call | solution.py:663
  189.5 0.0 copy-start
  189.5 3.2 %copy.15 = f32[2,512,512]{2,1,0:T(8,128)} copy(f32[2,512,512]{2,1,0:T(8,128)} %get-tuple-element.4) | data formatting | bytes 4194304
  192.7 0.0 copy-done
  192.7 1.3 copy.16
Async XLA Ops:
  189.5 3.2 %copy-start = (f32[2,512,512]{2,1,0:T(8,128)S(1)}, f32[2,512,512]{2,1,0:T(8,128)}, u32[]{:S(2)}) copy-start(f32[2,512,512]{2,1,0:T(8,128)} %get-tuple-element.5) | copy-start | bytes 6291460

commit v2 on v1

--- a/solution.py
+++ b/solution.py
@@ -14,7 +14,7 @@
 SLOTS = 3
 ROWS = 64
 CHUNKS = WIN // ROWS
-LAG = 2
+LAG = 1
 TILES = 8
 COLS = 16
 SEAM = 8
@@ -453,21 +453,30 @@
             def _():
                 grad_corner_direct(j).start()
 
+            @pl.when(before_seam)
+            def _():
+                grad_side(j).start()
+
         @pl.when(j >= LAG)
         def _():
             k = j - LAG
             add_down(k)
 
-            @pl.when(has_right)
-            def _():
-                grad_side(k).start()
-
         return carry
 
     lax.fori_loop(0, CHUNKS + LAG, backward_step, 0)
 
+    def send_side(k, carry):
+        @pl.when(has_right & jnp.logical_not(before_seam))
+        def _():
+            grad_side(k).start()
+
+        return carry
+
+    lax.fori_loop(0, CHUNKS, send_side, 0)
+
     def unroll_term(step, carry):
-        base = step * QUARTER
+        base = ((step // 2 + 1 - core) % 2) * (WIN // 2) + (step % 2) * QUARTER
         rows = pl.ds(pl.multiple_of(base, QUARTER), QUARTER)
         picks = [one_hot((QUARTER, WIN), 1, base, place[2 * s]) for s in range(SLOTS)]
         pick = jnp.concatenate(picks, axis=1)
@@ -476,43 +485,34 @@
             probe_sum[part, rows, :] = dot(pick, term_hi[:, columns]) + dot(pick, term_lo[:, columns])
         return carry
 
-    lax.fori_loop(0, 4, unroll_term, 0)
-
     half = WIN // 2
     mine = pl.multiple_of(core * half, half)
     theirs = pl.multiple_of((1 - core) * half, half)
-    pair_copy = remote(
-        probe_sum.at[:, pl.ds(theirs, half), :], pair_in, pair_s, pair_r, partner
-    )
-    pair_copy.start()
-    pair_copy.wait_recv()
-
-    def add_pair(k, carry):
-        for part in range(2):
-            rows = pl.ds(pl.multiple_of(mine + k * ROWS, ROWS), ROWS)
-            probe_sum[part, rows, :] += pair_in[part, chunk_rows(k), :]
-        return carry
-
-    lax.fori_loop(0, half // ROWS, add_pair, 0)
-
-    def z_copy(step):
+    z_rows = pl.ds(pl.multiple_of(mine + z * ROWS, ROWS), ROWS)
+
+    def pair_copy(part):
+        return remote(
+            probe_sum.at[part, pl.ds(theirs, half), :], pair_in.at[part], pair_s.at[part],
+            pair_r.at[part], partner,
+        )
+
+    lax.fori_loop(0, 2, unroll_term, 0)
+    for part in range(2):
+        pair_copy(part).start()
+    lax.fori_loop(2, 4, unroll_term, 0)
+
+    def z_copy(part, step):
         peer = (z + step) % 4
         rows = pl.ds(pl.multiple_of(mine + peer * ROWS, ROWS), ROWS)
         return remote(
-            probe_sum.at[:, rows, :], z_in.at[step - 1], z_s.at[step - 1], z_r.at[step - 1],
-            device_at(peer, y, x, core),
-        )
-
-    for step in (2, 1, 3):
-        z_copy(step).start()
-    z_rows = pl.ds(pl.multiple_of(mine + z * ROWS, ROWS), ROWS)
-    for step in (1, 2, 3):
-        z_copy(step).wait_recv()
-    for part in range(2):
-        probe_sum[part, z_rows, :] += z_in[0, part] + z_in[1, part] + z_in[2, part]
+            probe_sum.at[part, rows, :], z_in.at[part, step - 1], z_s.at[part, step - 1],
+            z_r.at[part, step - 1], device_at(peer, y, x, core),
+        )
 
     def piece(index):
         return index // 8, pl.ds(pl.multiple_of(mine + z * ROWS + (index % 8) * 8, 8), 8)
+
+    my_part, my_rows = piece(plane_me)
 
     def plane_copy(step):
         peer = (plane_me + step) % 16
@@ -522,12 +522,48 @@
             plane_r.at[step - 1], device_at(z, peer // 4, peer % 4, core),
         )
 
+    def gather_copy(step):
+        peer = (plane_me + step) % 16
+        return remote(
+            gathered.at[my_part, my_rows, :], gathered.at[my_part, my_rows, :],
+            ag_s.at[step - 1], ag_r.at[step - 1], device_at(z, peer // 4, peer % 4, core),
+        )
+
+    def z_gather(part, step):
+        peer = (z + step) % 4
+        return remote(
+            gathered.at[part, z_rows, :], gathered.at[part, z_rows, :], zg_s.at[part, step - 1],
+            zg_r.at[part, step - 1], device_at(peer, y, x, core),
+        )
+
+    def pair_gather(part):
+        rows = pl.ds(mine, half)
+        return remote(
+            gathered.at[part, rows, :], gathered.at[part, rows, :], pg_s.at[part], pg_r.at[part],
+            partner,
+        )
+
+    for part in range(2):
+        pair_copy(part).wait_recv()
+
+        def add_pair(k, carry):
+            rows = pl.ds(pl.multiple_of(mine + k * ROWS, ROWS), ROWS)
+            probe_sum[part, rows, :] += pair_in[part, chunk_rows(k), :]
+            return carry
+
+        lax.fori_loop(0, half // ROWS, add_pair, 0)
+        for step in (2, 1, 3):
+            z_copy(part, step).start()
+    for part in range(2):
+        for step in (1, 2, 3):
+            z_copy(part, step).wait_recv()
+        probe_sum[part, z_rows, :] += z_in[part, 0] + z_in[part, 1] + z_in[part, 2]
+
     def start_plane(step, carry):
         plane_copy(step).start()
         return carry
 
     lax.fori_loop(1, 16, start_plane, 0)
-    my_part, my_rows = piece(plane_me)
 
     def add_plane(step, total):
         plane_copy(step).wait_recv()
@@ -536,13 +572,6 @@
     total = lax.fori_loop(1, 16, add_plane, probe_sum[my_part, my_rows, :])
     gathered[my_part, my_rows, :] = total * (1.0 / (TILES * COLS * SLOTS))
 
-    def gather_copy(step):
-        peer = (plane_me + step) % 16
-        return remote(
-            gathered.at[my_part, my_rows, :], gathered.at[my_part, my_rows, :],
-            ag_s.at[step - 1], ag_r.at[step - 1], device_at(z, peer // 4, peer % 4, core),
-        )
-
     def start_gather(step, carry):
         gather_copy(step).start()
         return carry
@@ -553,23 +582,9 @@
 
     lax.fori_loop(1, 16, start_gather, 0)
     lax.fori_loop(1, 16, wait_gather, 0)
-
-    def z_gather(step):
-        peer = (z + step) % 4
-        return remote(
-            gathered.at[:, z_rows, :], gathered.at[:, z_rows, :], zg_s.at[step - 1],
-            zg_r.at[step - 1], device_at(peer, y, x, core),
-        )
-
-    for step in (2, 1, 3):
-        z_gather(step).start()
-    for step in (1, 2, 3):
-        z_gather(step).wait_recv()
-    pair_gather = remote(
-        gathered.at[:, pl.ds(mine, half), :], gathered.at[:, pl.ds(mine, half), :], pg_s, pg_r,
-        partner,
-    )
-    pair_gather.start()
+    for part in range(2):
+        for step in (2, 1, 3):
+            z_gather(part, step).start()
 
     def out_copy(k):
         rows = chunk_rows(k)
@@ -602,7 +617,12 @@
         return carry
 
     lax.fori_loop(0, CHUNKS, finish, 0)
-    pair_gather.wait_recv()
+    for part in range(2):
+        for step in (1, 2, 3):
+            z_gather(part, step).wait_recv()
+        pair_gather(part).start()
+    for part in range(2):
+        pair_gather(part).wait_recv()
     probe_out = pltpu.make_async_copy(gathered, out_probe, out_sem.at[CHUNKS])
     probe_out.start()
 
@@ -642,11 +662,12 @@
         return carry
 
     lax.fori_loop(1, 16, drain_plane, 0)
-    for step in (1, 2, 3):
-        z_copy(step).wait_send()
-        z_gather(step).wait_send()
-    pair_copy.wait_send()
-    pair_gather.wait_send()
+    for part in range(2):
+        for step in (1, 2, 3):
+            z_copy(part, step).wait_send()
+            z_gather(part, step).wait_send()
+        pair_copy(part).wait_send()
+        pair_gather(part).wait_send()
     probe_out.wait()
 
 
@@ -686,15 +707,15 @@
             pltpu.VMEM((2 * SLOTS * ROWS, 2 * WIN), BF16),
             pltpu.VMEM(block, F32),
             pltpu.VMEM((2, WIN // 2, WIN), F32),
-            pltpu.VMEM((3, 2, ROWS, WIN), F32),
+            pltpu.VMEM((2, 3, ROWS, WIN), F32),
             pltpu.VMEM((15, 8, WIN), F32),
             pltpu.VMEM(block, F32),
             dma((10,)), dma((CHUNKS + 1,)),
             dma((CHUNKS,)), dma((CHUNKS,)), dma((CHUNKS,)), dma((CHUNKS,)),
             dma((CHUNKS,)), dma((CHUNKS,)), dma((CHUNKS,)), dma((CHUNKS,)),
             dma((CHUNKS,)), dma((CHUNKS,)), dma((CHUNKS,)), dma((CHUNKS,)),
-            dma, dma, dma((3,)), dma((3,)), dma((15,)), dma((15,)),
-            dma((15,)), dma((15,)), dma((3,)), dma((3,)), dma, dma,
+            dma((2,)), dma((2,)), dma((2, 3)), dma((2, 3)), dma((15,)), dma((15,)),
+            dma((15,)), dma((15,)), dma((2, 3)), dma((2, 3)), dma((2,)), dma((2,)),
         ],
         compiler_params=pltpu.CompilerParams(
             collective_id=0, has_side_effects=True, vmem_limit_bytes=62 * 1024 * 1024

time: 194 us -> 191 us (0.985)
  Pallas kernels: 187 us -> 184 us
    pallas_call x1, Pallas kernels: 187 us -> 184 us  [on_device(): pl.pallas_call(kernel, name='ptycho_step', out_shape=(jax.ShapeDtypeStruc...]
where the time goes in v2:
time: 191 us
  Pallas kernels  184 us (96%)
  local copies, waits for them, and re-layouts  5.91 us (3%)
    pallas_call x1, Pallas kernels, on_device(): pl.pallas_call(kernel, name='ptycho_step', out_shape=(jax.ShapeDtypeStruc...  184 us
    unnamed x5, local copies, waits for them, and re-layouts  5.32 us

profile of v2, /device:TPU:1, one launch (start us, length us, event | category | flops | bytes accessed | tf_op | source)
XLA Modules:
  0.0 190.6 jit_solution(11611230782282574024)
XLA Ops:
  0.6 0.8 copy.12
  1.4 0.6 reshape.13.place
  2.0 184.0 %ptycho_step.1 = (f32[2,512,512]{2,1,0:T(8,128)}, f32[2,512,512]{2,1,0:T(8,128)}) custom-call(s32[6]{0:T(128)} %reshape.13.place, s32[16]{0:T(128)} %bitcast.3, f32[2,512,512]{2,1,0:T(8,128)} %obj.1, f32[2,512,512]{2,1,0:T(8,128)} %probe.1, f32[3,512,512]{2,1,0:T(8,128)} %bitcast.2, bf16[1024,512]{1,0:T(8,128)(2,1)} %constant.8.clone.row_hi, ...), custom_call_target="tpu_custom_call" | custom-call | flops 20000000000 | bytes 16000000 | tf_op jit(solution)/shard_map/ptycho_step/pallas_call | solution.py:684
  186.0 0.0 copy-start
  186.1 3.2 %copy.15 = f32[2,512,512]{2,1,0:T(8,128)} copy(f32[2,512,512]{2,1,0:T(8,128)} %get-tuple-element.4) | data formatting | bytes 4194304
  189.3 0.0 copy-done
  189.3 1.3 copy.16
Async XLA Ops:
  186.0 3.2 %copy-start = (f32[2,512,512]{2,1,0:T(8,128)S(1)}, f32[2,512,512]{2,1,0:T(8,128)}, u32[]{:S(2)}) copy-start(f32[2,512,512]{2,1,0:T(8,128)} %get-tuple-element.5) | copy-start | bytes 6291460

commit v3 on v2

--- a/solution.py
+++ b/solution.py
@@ -77,14 +77,14 @@
 
 def kernel(
     place, counts, obj, probe, inten, row_hi, row_lo, col_hi, col_lo,
-    out_obj, out_probe,
+    out_obj, out_probe, relay,
     own, halo, grad, back, spec, turned, term_hi, term_lo, roll_cols, unroll_cols, measured,
     wh, wl, ch, cl, left_hi, left_lo,
     probe_sum, pair_in, z_in, plane_in, gathered,
     load_sem, out_sem,
     up_s, up_r, side_s, side_r, cor_s, cor_r,
     gb_s, gb_r, gc_s, gc_r, gd_s, gd_r,
-    pair_s, pair_r, z_s, z_r, plane_s, plane_r, ag_s, ag_r, zg_s, zg_r, pg_s, pg_r,
+    ra_s, ra_r, rb_s, rb_r, rc_s, rc_r, rc_on, rd_s, rd_r, rd_on, pair_s, pair_r, z_s, z_r, plane_s, plane_r, ag_s, ag_r, zg_s, zg_r, pg_s, pg_r,
 ):
     t = lax.axis_index("tile")
     p = lax.axis_index("pos")
@@ -121,10 +121,15 @@
 
     t_up = (t + TILES - 1) % TILES
     t_down = (t + 1) % TILES
+    t_other = t + 1 - 2 * (t % 2)
     p_left = (p + COLS - 1) % COLS
     p_right = (p + 1) % COLS
     for device in (
         (t_up, p), (t_down, p), (t, p_left), (t, p_right), (t_up, p_left), (t_down, p_right),
+        (t_other, p), (t_other, p_left), (t_other, p_right),
+        ((t + TILES - 2) % TILES, p_right), ((t + 2) % TILES, p_left),
+        (t_down, (p + COLS - 2) % COLS), (t_up, (p + 2) % COLS),
+        ((t + TILES - 2) % TILES, p), ((t + 2) % TILES, p), (t_up, p_right), (t_down, p_left),
     ):
         greet(device)
     for step in range(1, 4):
@@ -136,7 +141,7 @@
         return carry
 
     lax.fori_loop(1, 16, greet_plane, 0)
-    pl.semaphore_wait(barrier, 6 + 3 + 15)
+    pl.semaphore_wait(barrier, 17 + 3 + 15)
 
     def remote(source, target, send, recv, device):
         return pltpu.make_async_remote_copy(
@@ -168,6 +173,60 @@
         return remote(
             obj.at[:, rows, :], halo.at[CORNER, :, rows, :], cor_s.at[k], cor_r.at[k],
             (t_up, p_left),
+        )
+
+    def detour(k):
+        rows = chunk_rows(k)
+        return remote(
+            obj.at[:, rows, :], relay.at[0, :, rows, :], ra_s.at[k], ra_r.at[k], (t_other, p_left)
+        )
+
+    def detour_on(k):
+        rows = chunk_rows(k)
+        return remote(
+            relay.at[0, :, rows, :], halo.at[RIGHT, :, rows, :], ra_s.at[k], side_r.at[k],
+            (t_other, p),
+        )
+
+    def corner_detour(k):
+        rows = chunk_rows(k)
+        return remote(
+            obj.at[:, rows, :], relay.at[1, :, rows, :], rb_s.at[k], rb_r.at[k],
+            ((t + TILES - 2) % TILES, p_right),
+        )
+
+    def corner_detour_on(k):
+        rows = chunk_rows(k)
+        return remote(
+            relay.at[1, :, rows, :], halo.at[CORNER, :, rows, :], rb_s.at[k], cor_r.at[k],
+            (t_down, (p + COLS - 2) % COLS),
+        )
+
+    def grad_detour(k):
+        rows = chunk_rows(k)
+        return remote(
+            grad.at[1, :, rows, :], relay.at[2, :, rows, :], rc_s.at[k], rc_r.at[k], (t_other, p)
+        )
+
+    def grad_detour_on(k):
+        rows = chunk_rows(k)
+        return remote(
+            relay.at[2, :, rows, :], back.at[RIGHT, :, rows, :], rc_on.at[k], gb_r.at[k],
+            (t_other, p_right),
+        )
+
+    def grad_corner_detour(k):
+        rows = chunk_rows(k)
+        return remote(
+            grad.at[3, :, rows, :], relay.at[3, :, rows, :], rd_s.at[k], rd_r.at[k],
+            ((t + 2) % TILES, p),
+        )
+
+    def grad_corner_detour_on(k):
+        rows = chunk_rows(k)
+        return remote(
+            relay.at[3, :, rows, :], back.at[CORNER, :, rows, :], rd_on.at[k], gd_r.at[k],
+            (t_up, p_right),
         )
 
     def grad_side(k):
@@ -204,6 +263,16 @@
     has_right = p < COLS - 1
     after_seam = p == SEAM
     before_seam = p == SEAM - 1
+    even = t % 2 == 0
+    turns_corner = even & has_up & after_seam
+    relays_corner = even & (t < TILES - 2) & (p == SEAM + 1)
+
+    turns_grad_corner = before_seam & has_down & jnp.logical_not(even)
+    relays_grad_corner = before_seam & (t > 2) & jnp.logical_not(even)
+
+    def on_detour(k):
+        return k % 2 == 1
+
     passes_on = has_left & has_down & jnp.logical_not(after_seam)
 
     def first_sends(k, carry):
@@ -211,13 +280,21 @@
         def _():
             up_copy(k).start()
 
-        @pl.when(has_left)
+        @pl.when(has_left & jnp.logical_not(after_seam & on_detour(k)))
         def _():
             side_copy(k).start()
 
-        @pl.when(has_up & after_seam)
+        @pl.when(after_seam & on_detour(k))
+        def _():
+            detour(k).start()
+
+        @pl.when(has_up & after_seam & jnp.logical_not(even))
         def _():
             corner_direct(k).start()
+
+        @pl.when(turns_corner)
+        def _():
+            corner_detour(k).start()
 
         return carry
 
@@ -309,6 +386,16 @@
     def forward_step(j, carry):
         @pl.when(j < CHUNKS)
         def _():
+            @pl.when(before_seam & on_detour(j))
+            def _():
+                detour(j).wait_recv()
+                detour_on(j).start()
+
+            @pl.when(relays_corner)
+            def _():
+                corner_detour(j).wait_recv()
+                corner_detour_on(j).start()
+
             @pl.when(has_down)
             def _():
                 up_copy(j).wait_recv()
@@ -449,17 +536,26 @@
             def _():
                 grad_corner(j).start()
 
-            @pl.when(has_down & before_seam)
+            @pl.when(has_down & before_seam & even)
             def _():
                 grad_corner_direct(j).start()
 
-            @pl.when(before_seam)
+            @pl.when(turns_grad_corner)
+            def _():
+                grad_corner_detour(j).start()
+
+            @pl.when(before_seam & jnp.logical_not(on_detour(j)))
             def _():
                 grad_side(j).start()
 
+            @pl.when(before_seam & on_detour(j))
+            def _():
+                grad_detour(j).start()
+
         @pl.when(j >= LAG)
         def _():
             k = j - LAG
+
             add_down(k)
 
         return carry
@@ -488,7 +584,13 @@
     half = WIN // 2
     mine = pl.multiple_of(core * half, half)
     theirs = pl.multiple_of((1 - core) * half, half)
-    z_rows = pl.ds(pl.multiple_of(mine + z * ROWS, ROWS), ROWS)
+    inner = z + 1 - 2 * (z % 2)
+    outer = 3 - z
+    z_peers = ((inner, outer), (outer, inner))
+    z_keeps = ((((z + 1) // 2) % 2, z // 2), (z // 2, z % 2))
+    z_base = []
+    for first, second in z_keeps:
+        z_base.append(pl.multiple_of(mine + first * QUARTER + second * ROWS, ROWS))
 
     def pair_copy(part):
         return remote(
@@ -501,16 +603,54 @@
         pair_copy(part).start()
     lax.fori_loop(2, 4, unroll_term, 0)
 
-    def z_copy(part, step):
-        peer = (z + step) % 4
-        rows = pl.ds(pl.multiple_of(mine + peer * ROWS, ROWS), ROWS)
-        return remote(
-            probe_sum.at[part, rows, :], z_in.at[part, step - 1], z_s.at[part, step - 1],
-            z_r.at[part, step - 1], device_at(peer, y, x, core),
+    def pass_detours(k, carry):
+        @pl.when(relays_grad_corner)
+        def _():
+            grad_corner_detour(k).wait_recv()
+            grad_corner_detour_on(k).start()
+
+        @pl.when(before_seam & on_detour(k))
+        def _():
+            grad_detour(k).wait_recv()
+            grad_detour_on(k).start()
+
+        return carry
+
+    lax.fori_loop(0, CHUNKS, pass_detours, 0)
+
+    def z_first(part):
+        first = pl.multiple_of(mine + (1 - z_keeps[part][0]) * QUARTER, QUARTER)
+        return remote(
+            probe_sum.at[part, pl.ds(first, QUARTER), :], z_in.at[part, pl.ds(0, QUARTER), :],
+            z_s.at[part, 0], z_r.at[part, 0], device_at(z_peers[part][0], y, x, core),
+        )
+
+    def z_second(part):
+        keep, second = z_keeps[part]
+        start = pl.multiple_of(mine + keep * QUARTER + (1 - second) * ROWS, ROWS)
+        return remote(
+            probe_sum.at[part, pl.ds(start, ROWS), :], z_in.at[part, pl.ds(QUARTER, ROWS), :],
+            z_s.at[part, 1], z_r.at[part, 1], device_at(z_peers[part][1], y, x, core),
+        )
+
+    def z_gather_first(part):
+        rows = pl.ds(z_base[part], ROWS)
+        return remote(
+            gathered.at[part, rows, :], gathered.at[part, rows, :], zg_s.at[part, 0],
+            zg_r.at[part, 0], device_at(z_peers[part][1], y, x, core),
+        )
+
+    def z_gather_second(part):
+        start = pl.multiple_of(mine + z_keeps[part][0] * QUARTER, QUARTER)
+        rows = pl.ds(start, QUARTER)
+        return remote(
+            gathered.at[part, rows, :], gathered.at[part, rows, :], zg_s.at[part, 1],
+            zg_r.at[part, 1], device_at(z_peers[part][0], y, x, core),
         )
 
     def piece(index):
-        return index // 8, pl.ds(pl.multiple_of(mine + z * ROWS + (index % 8) * 8, 8), 8)
+        base = jnp.where(index // 8 == 0, z_base[0], z_base[1])
+        return index // 8, pl.ds(pl.multiple_of(base + (index % 8) * 8, 8), 8)
 
     my_part, my_rows = piece(plane_me)
 
@@ -527,13 +667,6 @@
         return remote(
             gathered.at[my_part, my_rows, :], gathered.at[my_part, my_rows, :],
             ag_s.at[step - 1], ag_r.at[step - 1], device_at(z, peer // 4, peer % 4, core),
-        )
-
-    def z_gather(part, step):
-        peer = (z + step) % 4
-        return remote(
-            gathered.at[part, z_rows, :], gathered.at[part, z_rows, :], zg_s.at[part, step - 1],
-            zg_r.at[part, step - 1], device_at(peer, y, x, core),
         )
 
     def pair_gather(part):
@@ -552,12 +685,15 @@
             return carry
 
         lax.fori_loop(0, half // ROWS, add_pair, 0)
-        for step in (2, 1, 3):
-            z_copy(part, step).start()
+        z_first(part).start()
     for part in range(2):
-        for step in (1, 2, 3):
-            z_copy(part, step).wait_recv()
-        probe_sum[part, z_rows, :] += z_in[part, 0] + z_in[part, 1] + z_in[part, 2]
+        z_first(part).wait_recv()
+        kept = pl.multiple_of(mine + z_keeps[part][0] * QUARTER, QUARTER)
+        probe_sum[part, pl.ds(kept, QUARTER), :] += z_in[part, pl.ds(0, QUARTER), :]
+        z_second(part).start()
+    for part in range(2):
+        z_second(part).wait_recv()
+        probe_sum[part, pl.ds(z_base[part], ROWS), :] += z_in[part, pl.ds(QUARTER, ROWS), :]
 
     def start_plane(step, carry):
         plane_copy(step).start()
@@ -583,8 +719,10 @@
     lax.fori_loop(1, 16, start_gather, 0)
     lax.fori_loop(1, 16, wait_gather, 0)
     for part in range(2):
-        for step in (2, 1, 3):
-            z_gather(part, step).start()
+        z_gather_first(part).start()
+    for part in range(2):
+        z_gather_first(part).wait_recv()
+        z_gather_second(part).start()
 
     def out_copy(k):
         rows = chunk_rows(k)
@@ -618,8 +756,7 @@
 
     lax.fori_loop(0, CHUNKS, finish, 0)
     for part in range(2):
-        for step in (1, 2, 3):
-            z_gather(part, step).wait_recv()
+        z_gather_second(part).wait_recv()
         pair_gather(part).start()
     for part in range(2):
         pair_gather(part).wait_recv()
@@ -631,23 +768,52 @@
         def _():
             up_copy(k).wait_send()
 
-        @pl.when(has_left)
+        @pl.when(has_left & jnp.logical_not(after_seam & on_detour(k)))
         def _():
             side_copy(k).wait_send()
 
-        @pl.when(passes_on | (has_up & after_seam))
+        @pl.when(after_seam & on_detour(k))
+        def _():
+            detour(k).wait_send()
+
+        @pl.when(before_seam & on_detour(k))
+        def _():
+            detour_on(k).wait_send()
+
+        @pl.when(passes_on | (has_up & after_seam & jnp.logical_not(even)))
         def _():
             corner_copy(k).wait_send()
 
-        @pl.when(has_right)
+        @pl.when(turns_corner)
+        def _():
+            corner_detour(k).wait_send()
+
+        @pl.when(relays_corner)
+        def _():
+            corner_detour_on(k).wait_send()
+
+        @pl.when(has_right & jnp.logical_not(before_seam & on_detour(k)))
         def _():
             grad_side(k).wait_send()
 
+        @pl.when(before_seam & on_detour(k))
+        def _():
+            grad_detour(k).wait_send()
+            grad_detour_on(k).wait_send()
+
+        @pl.when(turns_grad_corner)
+        def _():
+            grad_corner_detour(k).wait_send()
+
+        @pl.when(relays_grad_corner)
+        def _():
+            grad_corner_detour_on(k).wait_send()
+
         @pl.when(has_down)
         def _():
             grad_down(k).wait_send()
 
-        @pl.when(has_right & has_down)
+        @pl.when(has_right & has_down & jnp.logical_not(turns_grad_corner))
         def _():
             grad_corner(k).wait_send()
 
@@ -663,9 +829,10 @@
 
     lax.fori_loop(1, 16, drain_plane, 0)
     for part in range(2):
-        for step in (1, 2, 3):
-            z_copy(part, step).wait_send()
-            z_gather(part, step).wait_send()
+        z_first(part).wait_send()
+        z_second(part).wait_send()
+        z_gather_first(part).wait_send()
+        z_gather_second(part).wait_send()
         pair_copy(part).wait_send()
         pair_gather(part).wait_send()
     probe_out.wait()
@@ -684,9 +851,12 @@
     return pl.pallas_call(
         kernel,
         name="ptycho_step",
-        out_shape=(jax.ShapeDtypeStruct(block, F32), jax.ShapeDtypeStruct(block, F32)),
+        out_shape=(
+            jax.ShapeDtypeStruct(block, F32), jax.ShapeDtypeStruct(block, F32),
+            jax.ShapeDtypeStruct((4,) + block, F32),
+        ),
         in_specs=[scalars, scalars] + [anywhere] * 7,
-        out_specs=(anywhere, anywhere),
+        out_specs=(anywhere, anywhere, anywhere),
         scratch_shapes=[
             pltpu.VMEM(block, F32),
             pltpu.VMEM((3,) + block, F32),
@@ -707,15 +877,18 @@
             pltpu.VMEM((2 * SLOTS * ROWS, 2 * WIN), BF16),
             pltpu.VMEM(block, F32),
             pltpu.VMEM((2, WIN // 2, WIN), F32),
-            pltpu.VMEM((2, 3, ROWS, WIN), F32),
+            pltpu.VMEM((2, QUARTER + ROWS, WIN), F32),
             pltpu.VMEM((15, 8, WIN), F32),
             pltpu.VMEM(block, F32),
             dma((10,)), dma((CHUNKS + 1,)),
             dma((CHUNKS,)), dma((CHUNKS,)), dma((CHUNKS,)), dma((CHUNKS,)),
             dma((CHUNKS,)), dma((CHUNKS,)), dma((CHUNKS,)), dma((CHUNKS,)),
             dma((CHUNKS,)), dma((CHUNKS,)), dma((CHUNKS,)), dma((CHUNKS,)),
-            dma((2,)), dma((2,)), dma((2, 3)), dma((2, 3)), dma((15,)), dma((15,)),
-            dma((15,)), dma((15,)), dma((2, 3)), dma((2, 3)), dma((2,)), dma((2,)),
+            dma((CHUNKS,)), dma((CHUNKS,)), dma((CHUNKS,)), dma((CHUNKS,)),
+            dma((CHUNKS,)), dma((CHUNKS,)), dma((CHUNKS,)),
+            dma((CHUNKS,)), dma((CHUNKS,)), dma((CHUNKS,)),
+            dma((2,)), dma((2,)), dma((2, 2)), dma((2, 2)), dma((15,)), dma((15,)),
+            dma((15,)), dma((15,)), dma((2, 2)), dma((2, 2)), dma((2,)), dma((2,)),
         ],
         compiler_params=pltpu.CompilerParams(
             collective_id=0, has_side_effects=True, vmem_limit_bytes=62 * 1024 * 1024
@@ -726,7 +899,7 @@
     )(
         place, count_row, object_field, probe_field, measured,
         jnp.asarray(row_hi), jnp.asarray(row_lo), jnp.asarray(col_hi), jnp.asarray(col_lo),
-    )
+    )[:2]
 
 
 def solution(mesh):

time: 191 us -> 189 us (0.990)
  Pallas kernels: 184 us -> 182 us
    pallas_call x1, Pallas kernels: 184 us -> 182 us  [on_device(): pl.pallas_call(kernel, name='ptycho_step', out_shape=(jax.ShapeDtypeStruc...]
where the time goes in v3:
time: 189 us; the launch traced here: 188 us
  Pallas kernels  182 us (96%)
  local copies, waits for them, and re-layouts  5.91 us (3%)
    pallas_call x1, Pallas kernels, on_device(): pl.pallas_call(kernel, name='ptycho_step', out_shape=(jax.ShapeDtypeStruc...  182 us
    unnamed x5, local copies, waits for them, and re-layouts  5.32 us

profile of v3, /device:TPU:1, one launch (start us, length us, event | category | flops | bytes accessed | tf_op | source)
XLA Modules:
  0.0 188.5 jit_solution(1960231989822361159)
XLA Ops:
  0.6 0.8 copy.12
  1.4 0.6 reshape.13.place
  2.0 181.9 %ptycho_step.1 = (f32[2,512,512]{2,1,0:T(8,128)}, f32[2,512,512]{2,1,0:T(8,128)}, f32[4,2,512,512]{3,2,1,0:T(8,128)}) custom-call(s32[6]{0:T(128)} %reshape.13.place, s32[16]{0:T(128)} %bitcast.3, f32[2,512,512]{2,1,0:T(8,128)} %obj.1, f32[2,512,512]{2,1,0:T(8,128)} %probe.1, f32[3,512,512]{2,1,0:T(8,128)} %bitcast.2, ...), custom_call_target="tpu_custom_call" | custom-call | flops 20000000000 | bytes 16000000 | tf_op jit(solution)/shard_map/ptycho_step/pallas_call | solution.py:851
  183.9 0.0 copy-start
  183.9 3.2 %copy.15 = f32[2,512,512]{2,1,0:T(8,128)} copy(f32[2,512,512]{2,1,0:T(8,128)} %get-tuple-element.8) | data formatting | bytes 4194304
  187.1 0.0 copy-done
  187.1 1.3 copy.16
Async XLA Ops:
  183.9 3.2 %copy-start = (f32[2,512,512]{2,1,0:T(8,128)S(1)}, f32[2,512,512]{2,1,0:T(8,128)}, u32[]{:S(2)}) copy-start(f32[2,512,512]{2,1,0:T(8,128)} %get-tuple-element.9) | copy-start | bytes 6291460

commit v4 on v3

--- a/solution.py
+++ b/solution.py
@@ -544,7 +544,7 @@
             def _():
                 grad_corner_detour(j).start()
 
-            @pl.when(before_seam & jnp.logical_not(on_detour(j)))
+            @pl.when(has_right & jnp.logical_not(before_seam & on_detour(j)))
             def _():
                 grad_side(j).start()
 
@@ -561,15 +561,6 @@
         return carry
 
     lax.fori_loop(0, CHUNKS + LAG, backward_step, 0)
-
-    def send_side(k, carry):
-        @pl.when(has_right & jnp.logical_not(before_seam))
-        def _():
-            grad_side(k).start()
-
-        return carry
-
-    lax.fori_loop(0, CHUNKS, send_side, 0)
 
     def unroll_term(step, carry):
         base = ((step // 2 + 1 - core) % 2) * (WIN // 2) + (step % 2) * QUARTER

time: 189 us -> 193 us (1.021)
  Pallas kernels: 182 us -> 185 us
    pallas_call x1, Pallas kernels: 182 us -> 185 us  [on_device(): pl.pallas_call(kernel, name='ptycho_step', out_shape=(jax.ShapeDtypeStruc...]
where the time goes in v4:
time: 193 us; the launch traced here: 192 us
  Pallas kernels  185 us (96%)
  local copies, waits for them, and re-layouts  5.91 us (3%)
    pallas_call x1, Pallas kernels, on_device(): pl.pallas_call(kernel, name='ptycho_step', out_shape=(jax.ShapeDtypeStruc...  185 us
    unnamed x5, local copies, waits for them, and re-layouts  5.32 us

profile of v4, /device:TPU:1, one launch (start us, length us, event | category | flops | bytes accessed | tf_op | source)
XLA Modules:
  0.0 192.0 jit_solution(13004378680399838970)
XLA Ops:
  0.6 0.8 copy.12
  1.4 0.6 reshape.13.place
  2.0 185.4 %ptycho_step.1 = (f32[2,512,512]{2,1,0:T(8,128)}, f32[2,512,512]{2,1,0:T(8,128)}, f32[4,2,512,512]{3,2,1,0:T(8,128)}) custom-call(s32[6]{0:T(128)} %reshape.13.place, s32[16]{0:T(128)} %bitcast.3, f32[2,512,512]{2,1,0:T(8,128)} %obj.1, f32[2,512,512]{2,1,0:T(8,128)} %probe.1, f32[3,512,512]{2,1,0:T(8,128)} %bitcast.2, ...), custom_call_target="tpu_custom_call" | custom-call | flops 20000000000 | bytes 16000000 | tf_op jit(solution)/shard_map/ptycho_step/pallas_call | solution.py:842
  187.4 0.0 copy-start
  187.4 3.2 %copy.15 = f32[2,512,512]{2,1,0:T(8,128)} copy(f32[2,512,512]{2,1,0:T(8,128)} %get-tuple-element.8) | data formatting | bytes 4194304
  190.6 0.0 copy-done
  190.6 1.3 copy.16
Async XLA Ops:
  187.4 3.2 %copy-start = (f32[2,512,512]{2,1,0:T(8,128)S(1)}, f32[2,512,512]{2,1,0:T(8,128)}, u32[]{:S(2)}) copy-start(f32[2,512,512]{2,1,0:T(8,128)} %get-tuple-element.9) | copy-start | bytes 6291460
